TPU v7x, 32 devices: a whole 2x2x4 slice. The times are simulated.
32 devices in a mesh: grp: 2 (over y), row: 16 (over z, x, core).
Axes of the slice: x: 2, y: 2, z: 4, core: 2. Of those that a mesh axis runs over, the one named last changes fastest.
Arguments:
- image: bfloat16 [128, 128, 3584], P(('grp', 'row')), parts along dimension 0, may hold values from -6 to 6
- mask: int32 [128, 2048], P(('grp', 'row')), parts along dimension 0, may hold values 0 or 1
- dictionary: bfloat16 [64, 4, 3584], replicated, may hold values from -0.046875 to 0.046875
- penalty: float32 [64], replicated, may hold values from 0.1 to 1
Outputs:
- codes: float32 [128, 128, 64], P(('grp', 'row')), parts along dimension 0
- grad_dict: float32 [7168, 256], P(('grp', 'row')), parts along dimension 0
There are 2 independent parts, one for each index of `grp`. A program takes and returns all parts, laid end to end along the dimension named above; an argument that names none is the same for every part. Nothing has to cross between parts.
All inputs are finite; a program needn't handle non-finite values. No bound on the sum of `mask` on one device may be relied on, other than what follows from the above.
Results may differ from a plain program's by a relative error of at most 0.0044.
Values may be sent and summed in bfloat16 or wider, within the bound.
A program may use at most 128 MiB of HBM per device.

v0:
```python
import math

import jax
import jax.numpy as jnp
from jax import lax
from jax.sharding import PartitionSpec as P

STEP_SIZE = 0.5


def passed_along(x, axis, by):
    devices = lax.axis_size(axis)
    pairs = [(i, i + by) for i in range(devices) if 0 <= i + by < devices]
    return lax.ppermute(x, axis, pairs)


def move_right(values):
    return jnp.concatenate([jnp.zeros_like(values[:, :1]), values[:, :-1]], axis=1)


def move_left(values):
    return jnp.concatenate([values[:, 1:], jnp.zeros_like(values[:, :1])], axis=1)


def local(image, mask, dictionary, penalty):
    block_rows, columns, features = image.shape
    atom_count = dictionary.shape[0]
    band_count = features // 16
    devices = lax.axis_size("row")
    scale = -1.0 / math.sqrt(block_rows * devices * columns)
    weight = mask.reshape(block_rows, columns, 16, 1).astype(jnp.float32)
    limit = STEP_SIZE * penalty

    def masked(values):
        shaped = values.reshape(block_rows, columns, 16, band_count)
        return (weight * shaped).reshape(block_rows, columns, features)

    def shrink(values):
        return values - jnp.clip(values, -limit, limit)

    def project(coded, quarter):
        height = coded.shape[0]
        flat = coded.reshape(height * columns, atom_count)
        result = jnp.dot(flat, dictionary[:, quarter], preferred_element_type=jnp.float32)
        return result.reshape(height, columns, features)

    def project_pair(coded, first):
        return project(coded, first) + move_right(project(coded, first + 1))

    def correlations(resid):
        height = resid.shape[0]
        flat = resid.reshape(height * columns, features)
        scores = jnp.einsum("rf,kqf->rqk", flat, dictionary, preferred_element_type=jnp.float32)
        scores = scores.reshape(height, columns, 4, atom_count)
        upper = scores[:, :, 0] + move_left(scores[:, :, 1])
        lower = scores[:, :, 2] + move_left(scores[:, :, 3])
        return (upper, lower)

    def fetch_below(resid):
        return passed_along(resid[0], "row", -1)

    def synthesize(coded):
        lower = project_pair(coded, 2)
        spilled = passed_along(lower[block_rows - 1], "row", 1)
        moved = jnp.concatenate([spilled[None], lower[: block_rows - 1]], axis=0)
        return (project_pair(coded, 0) + moved, coded)

    def analyze(resid):
        upper, lower = correlations(resid)
        extra_upper, extra_lower = correlations(fetch_below(resid)[None])
        return upper + jnp.concatenate([lower[1:], extra_lower], axis=0)

    pixels = image.astype(jnp.float32)
    start_resid = masked(pixels).astype(jnp.bfloat16)
    codes = shrink(STEP_SIZE * analyze(start_resid))
    approx, unused_rows = synthesize(codes.astype(jnp.bfloat16))
    resid = masked(pixels - approx).astype(jnp.bfloat16)
    codes = shrink(codes + STEP_SIZE * analyze(resid))
    rounded = codes.astype(jnp.bfloat16)
    approx, above = synthesize(rounded)
    final_resid = masked(pixels - approx).astype(jnp.bfloat16)
    extended = jnp.concatenate([final_resid, fetch_below(final_resid)[None]], axis=0)
    views = []
    for row_off in range(2):
        rows_now = extended[row_off : row_off + block_rows]
        views.append(rows_now.reshape(block_rows * columns, features))
        views.append(move_left(rows_now).reshape(block_rows * columns, features))
    flat_codes = rounded.reshape(block_rows * columns, atom_count)
    parts = [
        jnp.einsum("rf,rk->fk", view, flat_codes, preferred_element_type=jnp.float32)
        for view in views
    ]
    grad_dict = lax.psum_scatter(
        jnp.concatenate(parts, axis=1) * scale, "row", scatter_dimension=0, tiled=True
    )
    return (codes, grad_dict)


def solution(mesh):
    return jax.shard_map(
        local,
        mesh=mesh,
        in_specs=(P(("grp", "row"), None, None), P(("grp", "row"), None), P(), P()),
        out_specs=(P(("grp", "row"), None, None), P(("grp", "row"), None)),
        check_vma=False,
    )
```

profile of v0, /device:TPU:0, one launch (start us, length us, event | category | flops | bytes accessed | tf_op | source)
XLA Modules:
  0.0 233.8 jit_solution(6312929459782184264)
XLA Ops:
  8.2 3.5 %mul.43 = f32[4,128,16,224]{1,3,2,0:T(8,128)} broadcast(f32[4,128,16]{1,2,0:T(8,128)S(1)} %copy.44), dimensions={0,1,2} | broadcast | bytes 7372800 | tf_op jit(solution)/shard_map/mul | solution.py:36
  11.7 8.4 %copy.45 = f32[4,128,3584]{2,1,0:T(8,128)} copy(f32[4,128,3584]{1,2,0:T(8,128)} %bitcast.132) | data formatting | bytes 14680064 | tf_op jit(solution)/shard_map/mul | solution.py:36
  20.2 5.3 %fusion = bf16[4,128,3584]{2,1,0:T(8,128)(2,1)S(1)} fusion(f32[4,128,3584]{2,1,0:T(8,128)} %copy.45, bf16[4,128,3584]{2,1,0:T(8,128)(2,1)} %param.4), kind=kLoop, calls=%fused_computation.3 | loop fusion | flops 5505024 | bytes 14680064 | tf_op jit(solution)/shard_map/convert_element_type | solution.py:74
  25.5 1.3 collective-permute-start
  27.2 2.0 convolution_bitcast_fusion.5
  30.7 2.4 %convolution_bitcast_fusion.7 = f32[1,128,4,64]{1,3,2,0:T(8,128)S(1)} fusion(bf16[128,3584]{1,0:T(8,128)(2,1)} %collective-permute-done, bf16[64,4,3584]{2,1,0:T(4,128)(2,1)} %param.6), kind=kOutput, calls=%fused_computation.34 | convolution fusion | flops 234881024 | bytes 2883584 | tf_op jit(solution)/shard_map/rf,kqf->rqk/dot_general | solution.py:53
  35.8 14.4 %collective-permute-start.1 = (f32[128,3584]{1,0:T(8,128)S(1)}, f32[128,3584]{1,0:T(8,128)}, u32[]{:S(2)}, u32[]{:S(2)}) collective-permute-start(f32[128,3584]{1,0:T(8,128)S(1)} %slice_bitcast_fusion.1), channel_id=1, source_target_pairs={{0,1},{1,2},{2,3},{3,4},{4,5},{5,6},{6,7},{7,8},{8,9},{9,10},{10,1... | collective-permute-start | bytes 5505032 | tf_op jit(solution)/shard_map/ppermute | solution.py:14
  50.2 2.7 %slice.178 = f32[3,128,3584]{2,1,0:T(8,128)} slice(f32[4,128,3584]{2,1,0:T(8,128)S(1)} %pad_add_fusion.1), slice={[0:3], [0:128], [0:3584]} | slice | bytes 11010048 | tf_op jit(solution)/shard_map/slice | solution.py:65
  52.9 4.2 %fusion.20 = f32[4,127,3584]{2,1,0:T(8,128)} fusion(bf16[64,4,3584]{2,0,1:T(8,128)(2,1)S(1)} %copy.46, bf16[4,128,64]{1,2,0:T(8,128)(2,1)S(1)} %get-tuple-element.10), kind=kOutput, calls=%fused_computation.45 | convolution fusion | flops 233046016 | bytes 7806976 | tf_op jit(solution)/shard_map/dot_general | solution.py:44
  57.1 7.8 %fusion.2 = bf16[4,128,3584]{2,1,0:T(8,128)(2,1)} fusion(f32[4,128,3584]{2,1,0:T(8,128)S(1)} %bitcast.129, bf16[4,128,3584]{2,1,0:T(8,128)(2,1)S(1)} %copy-done, f32[3,128,3584]{2,1,0:T(8,128)} %slice.178, f32[1,128,3584]{2,1,0:T(8,128)} %bitcast.24, f32[4,127,3584]{2,1,0:T(8,128)} %fusion.20, bf16[4,128,64]{1,2,0:T(8,128)(2,1)S(1)} %get-tuple-element.10, ...), kind=kOutput, calls=%fused_computation.5 | convolution fusion | flops 247726080 | bytes 29827072 | tf_op jit(solution)/shard_map/dot_general | solution.py:44
  66.2 1.5 collective-permute-start.2
  67.6 4.6 %convolution_bitcast_fusion.4 = f32[512,4,64]{0,2,1:T(8,128)} fusion(bf16[512,3584,1]{1,0,2:T(8,128)(2,1)} %bitcast.133, bf16[64,4,3584]{2,1,0:T(4,128)(2,1)} %param.6), kind=kOutput, calls=%fused_computation.31 | convolution fusion | flops 939524096 | bytes 6029312 | tf_op jit(solution)/shard_map/rf,kqf->rqk/dot_general | solution.py:53
  73.8 8.6 %collective-permute-done.2 = bf16[128,3584]{1,0:T(8,128)(2,1)} collective-permute-done((bf16[128,3584]{1,0:T(8,128)(2,1)S(1)}, bf16[128,3584]{1,0:T(8,128)(2,1)}, u32[]{:S(2)}, u32[]{:S(2)}) %collective-permute-start.2) | collective-permute-done | bytes 917536 | tf_op jit(solution)/shard_map/ppermute | solution.py:14
  82.3 2.4 %convolution_bitcast_fusion.6 = f32[1,128,4,64]{1,3,2,0:T(8,128)S(1)} fusion(bf16[128,3584]{1,0:T(8,128)(2,1)} %collective-permute-done.2, bf16[64,4,3584]{2,1,0:T(4,128)(2,1)} %param.6), kind=kOutput, calls=%fused_computation.33 | convolution fusion | flops 234881024 | bytes 2883584 | tf_op jit(solution)/shard_map/rf,kqf->rqk/dot_general | solution.py:53
  88.1 14.0 %collective-permute-start.3 = (f32[128,3584]{1,0:T(8,128)S(1)}, f32[128,3584]{1,0:T(8,128)S(1)}, u32[]{:S(2)}, u32[]{:S(2)}) collective-permute-start(f32[128,3584]{1,0:T(8,128)S(1)} %slice_bitcast_fusion), channel_id=1, source_target_pairs={{0,1},{1,2},{2,3},{3,4},{4,5},{5,6},{6,7},{7,8},{8,9},{9,10},{10,1... | collective-permute-start | bytes 5505032 | tf_op jit(solution)/shard_map/ppermute | solution.py:14
  102.0 2.7 %slice.192 = f32[3,128,3584]{2,1,0:T(8,128)} slice(f32[4,128,3584]{2,1,0:T(8,128)S(1)} %pad_add_fusion), slice={[0:3], [0:128], [0:3584]} | slice | bytes 11010048 | tf_op jit(solution)/shard_map/slice | solution.py:65
  104.7 5.3 %fusion.19 = f32[4,127,3584]{2,1,0:T(8,128)} fusion(bf16[64,4,3584]{2,0,1:T(8,128)(2,1)} %copy-done.2, bf16[4,128,64]{1,2,0:T(8,128)(2,1)S(1)} %get-tuple-element.8), kind=kOutput, calls=%fused_computation.44 | convolution fusion | flops 233046016 | bytes 7806976 | tf_op jit(solution)/shard_map/dot_general | solution.py:44
  111.4 7.0 %fusion.4 = bf16[4,128,3584]{2,1,0:T(8,128)(2,1)S(1)} fusion(f32[4,128,3584]{2,1,0:T(8,128)S(1)} %bitcast.131, bf16[4,128,3584]{2,1,0:T(8,128)(2,1)S(1)} %copy-done.1, f32[3,128,3584]{2,1,0:T(8,128)} %slice.192, f32[1,128,3584]{2,1,0:T(8,128)} %bitcast.135, f32[4,127,3584]{2,1,0:T(8,128)} %fusion.19, bf16[4,128,64]{1,2,0:T(8,128)(2,1)S(1)} %get-tuple-element.8, ...), kind=kOutput, calls=%fused_computation.7 | convolution fusion | flops 247726080 | bytes 29884416 | tf_op jit(solution)/shard_map/dot_general | solution.py:44
  118.4 1.3 collective-permute-start.4
  122.0 12.4 %collective-permute-done.4 = bf16[128,3584]{1,0:T(8,128)(2,1)S(1)} collective-permute-done((bf16[128,3584]{1,0:T(8,128)(2,1)S(1)}, bf16[128,3584]{1,0:T(8,128)(2,1)S(1)}, u32[]{:S(2)}, u32[]{:S(2)}) %collective-permute-start.4) | collective-permute-done | bytes 917536 | tf_op jit(solution)/shard_map/ppermute | solution.py:14
  134.4 1.5 convolution_bitcast_fusion
  136.8 2.1 maximum_multiply_fusion
  138.9 5.1 %copy.65 = f32[3584,256]{1,0:T(8,128)} copy(f32[3584,256]{0,1:T(8,128)} %maximum_multiply_fusion) | data formatting | bytes 7340032
  144.1 82.9 %reduce-scatter.4.cloned.1.call-done = f32[224,256]{1,0:T(8,128)} async-done(((f32[3584,256]{1,0:T(8,128)}), f32[224,256]{1,0:T(8,128)}) %reduce-scatter.4.cloned.1.call-update) | async-done | bytes 229392
  (68 shorter events, 16.1 us)
Async XLA Ops:
  7.2 219.8 %reduce-scatter.4.cloned.1.call-start = ((), (), s32[]{:S(2)}) async-start(), calls=%async_computation.1 | async-start | bytes 3899392
  20.1 6.7 %copy-start.4 = (bf16[64,4,3584]{2,1,0:T(4,128)(2,1)S(1)}, bf16[64,4,3584]{2,1,0:T(4,128)(2,1)}, u32[]{:S(2)}) copy-start(bf16[64,4,3584]{2,1,0:T(4,128)(2,1)} %param.6) | copy-start | bytes 5505028
  25.5 5.2 %collective-permute-start = (bf16[128,3584]{1,0:T(8,128)(2,1)S(1)}, bf16[128,3584]{1,0:T(8,128)(2,1)}, u32[]{:S(2)}, u32[]{:S(2)}) collective-permute-start(bf16[128,3584]{1,0:T(8,128)(2,1)S(1)} %slice_bitcast_fusion.4), channel_id=1, source_target_pairs={{1,0},{2,1},{3,2},{4,3},{5,4},{6,5},{7,6},{8,7},{9,8},{10,9},{11,1... | collective-permute-start | bytes 2752520 | tf_op jit(solution)/shard_map/ppermute | solution.py:14
  27.2 59.6 %copy-start.2 = (bf16[64,4,3584]{2,0,1:T(8,128)(2,1)}, bf16[64,4,3584]{2,0,1:T(8,128)(2,1)S(1)}, u32[]{:S(2)}) copy-start(bf16[64,4,3584]{2,0,1:T(8,128)(2,1)S(1)} %copy.46) | copy-start | bytes 5505028
  27.2 3.5 %copy-start.5 = (f32[64]{0:T(128)S(1)}, f32[64]{0:T(128)}, u32[]{:S(2)}) copy-start(f32[64]{0:T(128)} %param.7) | copy-start | bytes 772
  35.7 21.4 %slice-start = ((s8[7340032]{0:T(1024)(128)(4,1)}), s8[4194304]{0:T(1024)(128)(4,1)S(1)}, s32[]{:S(2)}) async-start(s8[7340032]{0:T(1024)(128)(4,1)} %bitcast.128), calls=%async_computation.2 | async-start | bytes 8388608
  35.8 21.3 %slice-start.1 = ((s8[7340032]{0:T(1024)(128)(4,1)}), s8[3145728]{0:T(1024)(128)(4,1)S(1)}, s32[]{:S(2)}) async-start(s8[7340032]{0:T(1024)(128)(4,1)} %bitcast.128), calls=%async_computation.3 | async-start | bytes 6291456
  35.8 21.3 %collective-permute-start.1 = (f32[128,3584]{1,0:T(8,128)S(1)}, f32[128,3584]{1,0:T(8,128)}, u32[]{:S(2)}, u32[]{:S(2)}) collective-permute-start(f32[128,3584]{1,0:T(8,128)S(1)} %slice_bitcast_fusion.1), channel_id=1, source_target_pairs={{0,1},{1,2},{2,3},{3,4},{4,5},{5,6},{6,7},{7,8},{8,9},{9,10},{10,1... | collective-permute-start | bytes 5505032 | tf_op jit(solution)/shard_map/ppermute | solution.py:14
  52.9 4.2 %copy-start = (bf16[4,128,3584]{2,1,0:T(8,128)(2,1)S(1)}, bf16[4,128,3584]{2,1,0:T(8,128)(2,1)}, u32[]{:S(2)}) copy-start(bf16[4,128,3584]{2,1,0:T(8,128)(2,1)} %param.4) | copy-start | bytes 11010052
  66.2 16.2 %collective-permute-start.2 = (bf16[128,3584]{1,0:T(8,128)(2,1)S(1)}, bf16[128,3584]{1,0:T(8,128)(2,1)}, u32[]{:S(2)}, u32[]{:S(2)}) collective-permute-start(bf16[128,3584]{1,0:T(8,128)(2,1)S(1)} %slice_bitcast_fusion.3), channel_id=1, source_target_pairs={{1,0},{2,1},{3,2},{4,3},{5,4},{6,5},{7,6},{8,7},{9,8},{10,9},{11,1... | collective-permute-start | bytes 2752520 | tf_op jit(solution)/shard_map/ppermute | solution.py:14
  87.9 23.4 %slice-start.2 = ((s8[7340032]{0:T(1024)(128)(4,1)}), s8[4194304]{0:T(1024)(128)(4,1)S(1)}, s32[]{:S(2)}) async-start(s8[7340032]{0:T(1024)(128)(4,1)} %bitcast.130), calls=%async_computation.4 | async-start | bytes 8388608
  88.1 23.3 %slice-start.3 = ((s8[7340032]{0:T(1024)(128)(4,1)}), s8[3145728]{0:T(1024)(128)(4,1)S(1)}, s32[]{:S(2)}) async-start(s8[7340032]{0:T(1024)(128)(4,1)} %bitcast.130), calls=%async_computation.5 | async-start | bytes 6291456
  88.1 22.0 %collective-permute-start.3 = (f32[128,3584]{1,0:T(8,128)S(1)}, f32[128,3584]{1,0:T(8,128)S(1)}, u32[]{:S(2)}, u32[]{:S(2)}) collective-permute-start(f32[128,3584]{1,0:T(8,128)S(1)} %slice_bitcast_fusion), channel_id=1, source_target_pairs={{0,1},{1,2},{2,3},{3,4},{4,5},{5,6},{6,7},{7,8},{8,9},{9,10},{10,1... | collective-permute-start | bytes 5505032 | tf_op jit(solution)/shard_map/ppermute | solution.py:14
  104.7 6.6 %copy-start.1 = (bf16[4,128,3584]{2,1,0:T(8,128)(2,1)S(1)}, bf16[4,128,3584]{2,1,0:T(8,128)(2,1)}, u32[]{:S(2)}) copy-start(bf16[4,128,3584]{2,1,0:T(8,128)(2,1)} %param.4) | copy-start | bytes 11010052
  110.1 1.3 copy-start.3
  118.4 16.0 %collective-permute-start.4 = (bf16[128,3584]{1,0:T(8,128)(2,1)S(1)}, bf16[128,3584]{1,0:T(8,128)(2,1)S(1)}, u32[]{:S(2)}, u32[]{:S(2)}) collective-permute-start(bf16[128,3584]{1,0:T(8,128)(2,1)S(1)} %slice_bitcast_fusion.2), channel_id=1, source_target_pairs={{1,0},{2,1},{3,2},{4,3},{5,4},{6,5},{7,6},{8,7},{9,8},{10,9},{11,1... | collective-permute-start | bytes 2752520 | tf_op jit(solution)/shard_map/ppermute | solution.py:14
Sparse Core Ops, SparseCore 0:
  144.2 82.7 reduce-scatter.3
where the time goes:
time: 234 us
  waiting for transfers between devices  104 us (44%)
  matrix products  44.2 us (19%)
  starting transfers between devices  32.4 us (14%)
  local copies, waits for them, and re-layouts  29.8 us (13%)
  between operations  14.4 us (6%)
  other arithmetic  9.1 us (4%)
    unnamed x2, waiting for transfers between devices  82.9 us
    ppermute x5, starting transfers between devices, passed_along(): return lax.ppermute(x, axis, pairs)  32.4 us
    dot_general x8, matrix products, project(): jnp.dot(flat, dictionary[:, quarter], preferred_element_type=jnp.float32)  28.8 us
    ppermute x5, waiting for transfers between devices, passed_along(): return lax.ppermute(x, axis, pairs)  20.9 us
    mul x2, local copies, waits for them, and re-layouts, masked(): return (weight * shaped).reshape(block_rows, columns, features)  11.9 us
    dot_general x4, matrix products, correlations(): jnp.einsum('rf,kqf->rqk', flat, dictionary, preferred_element_type=jnp.fl...  11.4 us
    unnamed x26, local copies, waits for them, and re-layouts  6.78 us
    slice x2, local copies, waits for them, and re-layouts, synthesize(): moved = jnp.concatenate([spilled[None], lower[:block_rows - 1]], axis=0)  5.4 us
  transfers between devices with their start and end apart: 6, of which 3 were waited for; matrix products, arithmetic and copies ran while one was open for 12% of the time, Pallas kernels for 0%

commit v1 on v0

v1 whole, which is shorter than its diff:
```python
import functools
import math

import jax
import jax.numpy as jnp
from jax import lax
from jax.experimental import pallas as pl
from jax.experimental.pallas import tpu as pltpu
from jax.sharding import PartitionSpec as P

STEP_SIZE = 0.5
QUAD = 4
F32 = jnp.float32
BF16 = jnp.bfloat16


def chunk_of(step, mine, quads):
    if quads == 4:
        return (3 - mine, (mine + 2) % 4, mine + 1 - 2 * (mine % 2), mine)[step]
    return (mine + 1 + step) % quads


def kernel(
    devices, block_rows, columns, fused,
    image_hbm, mask_ref, dict_hbm, penalty_ref,
    codes_ref, grad_ref,
    img, dic, weight, resid, spread, totals, low_out, low_in, wide, wide_in,
    partial, core_out, core_in, side_out, side_in, far_out, far_in,
    image_sem, dict_sem, low_send, low_recv, wide_send, wide_recv,
    core_send, core_recv, side_send, side_recv, far_send, far_recv,
):
    grp = lax.axis_index("grp")
    me = lax.axis_index("row")
    total_rows, features = img.shape
    bands = features // 16
    scale = -1.0 / math.sqrt(block_rows * devices * columns)
    quads = devices // QUAD
    core, side, far = me % 2, (me // 2) % 2, me // QUAD
    sibling = me + 1 - 2 * core
    beside = me + 2 - 4 * side
    first, last = slice(0, columns), slice(total_rows - columns, total_rows)

    def to(index):
        return dict(device_id=(grp, index), device_id_type=pl.DeviceIdType.MESH)

    barrier = pltpu.get_barrier_semaphore()

    @pl.when(me > 0)
    def _():
        pl.semaphore_signal(barrier, inc=1, **to(me - 1))

    @pl.when(me < devices - 1)
    def _():
        pl.semaphore_signal(barrier, inc=1, **to(me + 1))

    if fused:
        pl.semaphore_signal(barrier, inc=1, **to(beside))
        for step in range(quads - 1):
            other = chunk_of(step, far, quads) * QUAD + 2 * side + core
            pl.semaphore_signal(barrier, inc=1, **to(other))

    load_dict = pltpu.make_async_copy(dict_hbm, dic, dict_sem)
    load_image = pltpu.make_async_copy(image_hbm, img, image_sem)
    load_image.start()
    load_dict.start()

    @pl.when(me == 0)
    def _():
        wide_in[...] = jnp.zeros_like(wide_in)

    @pl.when(me == devices - 1)
    def _():
        low_in[...] = jnp.zeros_like(low_in)

    lane = lax.broadcasted_iota(jnp.int32, (8, 128), 1) // 16
    keep = lane == lax.broadcasted_iota(jnp.int32, (8, 128), 0)
    for i in range(block_rows):
        for j in range(columns // 8):
            flags = mask_ref[i : i + 1, j * 128 : (j + 1) * 128].astype(F32)
            spread[i * columns + j * 8 : i * columns + (j + 1) * 8, :] = jnp.where(
                keep, jnp.broadcast_to(flags, (8, 128)), 0.0
            )
    load_image.wait()

    width = 512 if features % 512 == 0 else 128

    def cut(index, size):
        return pl.ds(pl.multiple_of(index * size, 128), size)

    def start_chunk(index, carry):
        here = cut(index, width)
        place = lax.broadcasted_iota(jnp.int32, (128, width), 1) + index * width
        begin = (lax.broadcasted_iota(jnp.int32, (128, width), 0) % 16) * bands
        inside = (place >= begin) & (place < begin + bands)
        expand = jnp.where(inside, 1.0, 0.0).astype(BF16)
        spots = jnp.dot(spread[...].astype(BF16), expand, preferred_element_type=F32)
        spots = spots.astype(BF16)
        weight[:, here] = spots
        resid[:, here] = img[:, here] * spots
        return carry

    lax.fori_loop(0, features // width, start_chunk, 0)
    load_dict.wait()
    above = (me + devices - 1) // devices
    below = (2 * devices - 2 - me) // devices
    pl.semaphore_wait(barrier, above + below + (quads if fused else 0))

    limit = STEP_SIZE * penalty_ref[...]

    def scores(rows):
        return lax.dot_general(
            resid[rows, :], dic[...], (((1,), (1,)), ((), ())), preferred_element_type=F32
        )

    def low_copy(sweep):
        return pltpu.make_async_remote_copy(
            low_out.at[sweep], low_in.at[sweep], low_send.at[sweep], low_recv.at[sweep], **to(me - 1)
        )

    def wide_copy(sweep):
        return pltpu.make_async_remote_copy(
            wide.at[sweep, last], wide_in.at[sweep], wide_send.at[sweep], wide_recv.at[sweep], **to(me + 1)
        )

    def update(sweep, rows, sums):
        count = sums.shape[0]
        column = lax.broadcasted_iota(jnp.int32, (count, 128), 0) % columns
        moved = jnp.where(column == columns - 1, 0.0, pltpu.roll(sums, count - 1, 0))
        found = STEP_SIZE * (sums[:, :64] + moved[:, 64:])
        if sweep > 0:
            found = codes_ref[rows, :] + found
        found = found - jnp.clip(found, -limit, limit)
        codes_ref[rows, :] = found
        both = jnp.concatenate([found, found], axis=1)
        shifted = jnp.where(column == 0, 0.0, pltpu.roll(both, 1, 0))
        half = lax.broadcasted_iota(jnp.int32, (count, 128), 1) < 64
        wide[sweep, rows, :] = jnp.where(half, both, shifted).astype(BF16)

    def analyze(sweep):
        found = scores(first)
        low_out[sweep] = found[:, 128:]

        @pl.when(me > 0)
        def _():
            low_copy(sweep).start()

        totals[first, :] = found[:, :128]
        rest = scores(slice(columns, total_rows))
        totals[columns:, :] = rest[:, :128]
        upto = total_rows - columns
        update(sweep, slice(0, upto), totals[:upto, :] + rest[:, 128:])

        @pl.when(me < devices - 1)
        def _():
            low_copy(sweep).wait_recv()

        update(sweep, last, totals[last, :] + low_in[sweep])

        @pl.when(me < devices - 1)
        def _():
            wide_copy(sweep).start()

    def fold(sweep, which):
        if which == "rest":
            return jnp.concatenate(
                [wide[sweep, columns:, :], wide[sweep, : total_rows - columns, :]], axis=1
            )
        return jnp.concatenate([wide[sweep, first, :], wide_in[sweep]], axis=1)

    def residual(sweep, rows, which, here):
        approx = jnp.dot(fold(sweep, which), dic[:, here], preferred_element_type=F32)
        diff = img[rows, here].astype(F32) - approx
        resid[rows, here] = diff.astype(BF16) * weight[rows, here]

    analyze(0)

    def rest_chunk(index, carry):
        residual(0, slice(columns, total_rows), "rest", cut(index, width))
        return carry

    def first_chunk(index, carry):
        residual(0, first, "first", cut(index, width))
        return carry

    def await_above(sweep):
        @pl.when(me > 0)
        def _():
            wide_copy(sweep).wait_recv()

    lax.fori_loop(0, features // width, rest_chunk, 0)
    await_above(0)
    lax.fori_loop(0, features // width, first_chunk, 0)
    analyze(1)

    chunk = features // quads if fused else features // 4
    own = chunk // QUAD

    def gradient(here):
        residual(1, slice(columns, total_rows), "rest", here)
        residual(1, first, "first", here)
        codes = jnp.concatenate([fold(1, "first"), fold(1, "rest")], axis=0)
        found = lax.dot_general(
            resid[:, here], codes, (((0,), (0,)), ((), ())), preferred_element_type=F32
        )
        return found * scale

    await_above(1)
    if not fused:
        for step in range(4):
            grad_ref[step * chunk : (step + 1) * chunk, :] = gradient(cut(step, chunk))
    else:
        def piece(step, index):
            return partial[step, pl.ds(pl.multiple_of(index * own, 16), own), :]

        def core_copy(step):
            return pltpu.make_async_remote_copy(
                core_out.at[step], core_in.at[step], core_send.at[step], core_recv.at[step], **to(sibling)
            )

        def side_copy(step):
            return pltpu.make_async_remote_copy(
                side_out.at[step], side_in.at[step], side_send.at[step], side_recv.at[step], **to(beside)
            )

        def far_copy(step):
            owner = chunk_of(step, far, quads) * QUAD + 2 * side + core
            return pltpu.make_async_remote_copy(
                far_out.at[step], far_in.at[step], far_send.at[step], far_recv.at[step], **to(owner)
            )

        def stage_core(step):
            partial[step] = gradient(cut(chunk_of(step, far, quads), chunk))
            for across in range(2):
                core_out[step, across] = piece(step, 2 * across + 1 - core).astype(BF16)
            core_copy(step).start()

        def stage_side(step):
            core_copy(step).wait_recv()
            across = 1 - side
            side_out[step] = (piece(step, 2 * across + core) + core_in[step, across].astype(F32)).astype(BF16)
            side_copy(step).start()

        def summed(step):
            side_copy(step).wait_recv()
            mine = piece(step, 2 * side + core) + core_in[step, side].astype(F32)
            return mine + side_in[step].astype(F32)

        def stage_far(step):
            far_out[step] = summed(step).astype(BF16)
            far_copy(step).start()

        for step in range(quads):
            stage_core(step)
            if step >= 1:
                stage_side(step - 1)
            if step >= 2:
                stage_far(step - 2)
        stage_side(quads - 1)
        if quads >= 2:
            stage_far(quads - 2)
        result = summed(quads - 1)
        for step in range(quads - 1):
            far_copy(step).wait_recv()
            result = result + far_in[step].astype(F32)
        grad_ref[...] = result
        for step in range(quads):
            core_copy(step).wait_send()
            side_copy(step).wait_send()
            if step < quads - 1:
                far_copy(step).wait_send()

    for sweep in range(2):
        @pl.when(me > 0)
        def _():
            low_copy(sweep).wait_send()

        @pl.when(me < devices - 1)
        def _():
            wide_copy(sweep).wait_send()


def local(devices, image, mask, dictionary, penalty):
    block_rows, columns, features = image.shape
    atoms = dictionary.shape[0]
    rows = block_rows * columns
    quads = devices // QUAD
    fused = devices % QUAD == 0 and features % (quads * 128) == 0 and features // devices % 16 == 0
    own = features // devices
    slots = (quads, own) if fused else (1, 16)
    flat = jnp.transpose(dictionary, (1, 0, 2)).reshape(4 * atoms, features)
    dma, vmem = pltpu.SemaphoreType.DMA, pltpu.VMEM
    near, there = pl.BlockSpec(memory_space=pltpu.VMEM), pl.BlockSpec(memory_space=pl.ANY)
    codes, grad = pl.pallas_call(
        functools.partial(kernel, devices, block_rows, columns, fused),
        out_shape=(
            jax.ShapeDtypeStruct((rows, atoms), F32),
            jax.ShapeDtypeStruct((own if fused else features, 4 * atoms), F32),
        ),
        in_specs=[there, near, there, near],
        out_specs=(near, near),
        scratch_shapes=[
            vmem((rows, features), BF16),
            vmem((4 * atoms, features), BF16),
            vmem((rows, features), BF16),
            vmem((rows, features), BF16),
            vmem((rows, 128), F32),
            vmem((rows, 128), F32),
            vmem((2, columns, 128), F32),
            vmem((2, columns, 128), F32),
            vmem((2, rows, 128), BF16),
            vmem((2, columns, 128), BF16),
            vmem((slots[0], QUAD * slots[1], 4 * atoms), F32),
            vmem((slots[0], 2, slots[1], 4 * atoms), BF16),
            vmem((slots[0], 2, slots[1], 4 * atoms), BF16),
            vmem((slots[0], slots[1], 4 * atoms), BF16),
            vmem((slots[0], slots[1], 4 * atoms), BF16),
            vmem((slots[0], slots[1], 4 * atoms), BF16),
            vmem((slots[0], slots[1], 4 * atoms), BF16),
            dma, dma,
            dma((2,)), dma((2,)), dma((2,)), dma((2,)),
            dma((slots[0],)), dma((slots[0],)), dma((slots[0],)),
            dma((slots[0],)), dma((slots[0],)), dma((slots[0],)),
        ],
        compiler_params=pltpu.CompilerParams(
            collective_id=0, has_side_effects=True, vmem_limit_bytes=56 * 1024 * 1024
        ),
    )(image.reshape(rows, features), mask, flat, penalty.reshape(1, atoms))
    if not fused:
        grad = lax.psum_scatter(grad, "row", scatter_dimension=0, tiled=True)
    return (codes.reshape(block_rows, columns, atoms), grad)


def solution(mesh):
    return jax.shard_map(
        functools.partial(local, mesh.shape["row"]),
        mesh=mesh,
        in_specs=(P(("grp", "row"), None, None), P(("grp", "row"), None), P(), P()),
        out_specs=(P(("grp", "row"), None, None), P(("grp", "row"), None)),
        check_vma=False,
    )
```

time: 234 us -> 50.6 us (0.22)
  waiting for transfers between devices: 104 us -> 0 us
  matrix products: 44.2 us -> 0 us
  Pallas kernels: 0 us -> 43.3 us
  starting transfers between devices: 32.4 us -> 0 us
  local copies, waits for them, and re-layouts: 29.8 us -> 6.43 us
  between operations: 14.4 us -> 0.64 us
  other arithmetic: 9.1 us -> 0 us
    unnamed x2 -> x0, waiting for transfers between devices: 82.9 us -> none
    dot_general x16 -> x0, matrix products: 44.2 us -> none  [the longest x8 28.8 us: project(): jnp.dot(flat, dictionary[:, quarter], preferred_element_type=jnp.float32)]
    pallas_call x0 -> x1, Pallas kernels: none -> 43.3 us  [local(): pl.pallas_call(functools.partial(kernel, devices, block_rows, columns, fu...]
    ppermute x5 -> x0, starting transfers between devices: 32.4 us -> none  [passed_along(): return lax.ppermute(x, axis, pairs)]
    ppermute x5 -> x0, waiting for transfers between devices: 20.9 us -> none  [passed_along(): return lax.ppermute(x, axis, pairs)]
    mul x2 -> x0, local copies, waits for them, and re-layouts: 11.9 us -> none  [masked(): return (weight * shaped).reshape(block_rows, columns, features)]
    convert_element_type x4 -> x0, other arithmetic: 6.94 us -> none  [the longest x1 5.33 us: local(): start_resid = masked(pixels).astype(jnp.bfloat16)]
    slice x11 -> x0, local copies, waits for them, and re-layouts: 6.83 us -> none  [the longest x2 5.4 us: synthesize(): moved = jnp.concatenate([spilled[None], lower[:block_rows - 1]], axis=0)]
  transfers between devices with their start and end apart: 6 -> 0, of which waited for: 3 -> 0; matrix products, arithmetic and copies ran while one was open for 12% -> 0% of each run, Pallas kernels for 0% -> 0%
where the time goes in v1:
time: 50.6 us; the launch traced here: 50.3 us
  Pallas kernels  43.3 us (86%)
  local copies, waits for them, and re-layouts  6.43 us (13%)
  between operations  0.64 us (1%)
    pallas_call x1, Pallas kernels, local(): pl.pallas_call(functools.partial(kernel, devices, block_rows, columns, fu...  43.3 us
    unnamed x2, local copies, waits for them, and re-layouts  3.36 us
    transpose x1, local copies, waits for them, and re-layouts, local(): flat = jnp.transpose(dictionary, (1, 0, 2)).reshape(4 * atoms, features)  3.06 us

profile of v1, /device:TPU:0, one launch (start us, length us, event | category | flops | bytes accessed | tf_op | source)
XLA Modules:
  0.0 50.3 jit_solution(7706744325077931328)
XLA Ops:
  0.6 3.1 %copy.6 = bf16[4,64,3584]{2,1,0:T(8,128)(2,1)} copy(bf16[4,64,3584]{2,0,1:T(4,128)(2,1)} %bitcast.7) | data formatting | bytes 3670016 | tf_op jit(solution)/shard_map/transpose | solution.py:290
  3.7 43.3 %shard_map.59 = (f32[512,64]{1,0:T(8,128)}, f32[224,256]{1,0:T(8,128)}) custom-call(bf16[512,3584]{1,0:T(8,128)(2,1)} %bitcast.6, s32[4,2048]{1,0:T(4,128)} %mask_ref.1, bf16[256,3584]{1,0:T(8,128)(2,1)} %bitcast.5, f32[1,64]{1,0:T(1,128)} %bitcast.9), custom_call_target="tpu_custom_call" | custom-call | tf_op jit(solution)/shard_map/pallas_call | solution.py:293
  47.0 1.7 %copy.7 = f32[4,128,64]{1,2,0:T(8,128)} copy(f32[4,128,64]{2,1,0:T(8,128)} %bitcast.8) | data formatting | bytes 262144
  48.7 1.6 %copy.9 = f32[224,256]{1,0:T(8,128)} copy(f32[224,256]{1,0:T(8,128)} %get-tuple-element.11) | data formatting | bytes 458752

commit v2 on v1

--- a/solution.py
+++ b/solution.py
@@ -20,11 +20,15 @@
     return (mine + 1 + step) % quads
 
 
+def target_of(step, mine, quads):
+    return chunk_of(2 if quads == 4 and step == 0 else step, mine, quads)
+
+
 def kernel(
     devices, block_rows, columns, fused,
     image_hbm, mask_ref, dict_hbm, penalty_ref,
-    codes_ref, grad_ref,
-    img, dic, weight, resid, spread, totals, low_out, low_in, wide, wide_in,
+    codes_out, grad_ref,
+    codes_ref, raw, img, dic, weight, resid, spread, totals, low_out, low_in, wide, wide_in,
     partial, core_out, core_in, side_out, side_in, far_out, far_in,
     image_sem, dict_sem, low_send, low_recv, wide_send, wide_recv,
     core_send, core_recv, side_send, side_recv, far_send, far_recv,
@@ -55,14 +59,20 @@
 
     if fused:
         pl.semaphore_signal(barrier, inc=1, **to(beside))
-        for step in range(quads - 1):
+        for step in range(1 if quads == 4 else 0, quads - 1):
             other = chunk_of(step, far, quads) * QUAD + 2 * side + core
             pl.semaphore_signal(barrier, inc=1, **to(other))
 
-    load_dict = pltpu.make_async_copy(dict_hbm, dic, dict_sem)
-    load_image = pltpu.make_async_copy(image_hbm, img, image_sem)
-    load_image.start()
+    peers = 3 if quads == 4 else quads
+    load_dict = pltpu.make_async_copy(dict_hbm, raw, dict_sem)
+    load_first = pltpu.make_async_copy(
+        image_hbm.at[pl.ds(0, columns)], img.at[pl.ds(0, columns)], image_sem.at[0]
+    )
+    others = pl.ds(columns, total_rows - columns)
+    load_rest = pltpu.make_async_copy(image_hbm.at[others], img.at[others], image_sem.at[1])
     load_dict.start()
+    load_first.start()
+    load_rest.start()
 
     @pl.when(me == 0)
     def _():
@@ -80,8 +90,6 @@
             spread[i * columns + j * 8 : i * columns + (j + 1) * 8, :] = jnp.where(
                 keep, jnp.broadcast_to(flags, (8, 128)), 0.0
             )
-    load_image.wait()
-
     width = 512 if features % 512 == 0 else 128
 
     def cut(index, size):
@@ -92,18 +100,19 @@
         place = lax.broadcasted_iota(jnp.int32, (128, width), 1) + index * width
         begin = (lax.broadcasted_iota(jnp.int32, (128, width), 0) % 16) * bands
         inside = (place >= begin) & (place < begin + bands)
-        expand = jnp.where(inside, 1.0, 0.0).astype(BF16)
-        spots = jnp.dot(spread[...].astype(BF16), expand, preferred_element_type=F32)
-        spots = spots.astype(BF16)
-        weight[:, here] = spots
-        resid[:, here] = img[:, here] * spots
+        picked = jnp.where(inside, 1.0, 0.0).astype(BF16)
+        spots = jnp.dot(spread[...].astype(BF16), picked, preferred_element_type=F32)
+        weight[:, here] = spots.astype(BF16)
         return carry
 
     lax.fori_loop(0, features // width, start_chunk, 0)
     load_dict.wait()
+    atoms = raw.shape[0]
+    for quarter in range(4):
+        dic[quarter * atoms : (quarter + 1) * atoms, :] = raw[:, quarter, :]
     above = (me + devices - 1) // devices
     below = (2 * devices - 2 - me) // devices
-    pl.semaphore_wait(barrier, above + below + (quads if fused else 0))
+    pl.semaphore_wait(barrier, above + below + (peers if fused else 0))
 
     limit = STEP_SIZE * penalty_ref[...]
 
@@ -122,29 +131,49 @@
             wide.at[sweep, last], wide_in.at[sweep], wide_send.at[sweep], wide_recv.at[sweep], **to(me + 1)
         )
 
-    def update(sweep, rows, sums):
+    def lift(values):
+        count = values.shape[0]
+        column = lax.broadcasted_iota(jnp.int32, values.shape, 0) % columns
+        return jnp.where(column == columns - 1, 0.0, pltpu.roll(values, count - 1, 0))
+
+    def update(sweep, rows, sums, extra=None):
         count = sums.shape[0]
         column = lax.broadcasted_iota(jnp.int32, (count, 128), 0) % columns
-        moved = jnp.where(column == columns - 1, 0.0, pltpu.roll(sums, count - 1, 0))
-        found = STEP_SIZE * (sums[:, :64] + moved[:, 64:])
+        found = sums[:, :64] + lift(sums)[:, 64:]
+        if extra is not None:
+            found = found + extra
+        found = STEP_SIZE * found
         if sweep > 0:
             found = codes_ref[rows, :] + found
         found = found - jnp.clip(found, -limit, limit)
-        codes_ref[rows, :] = found
+        if sweep == 0:
+            codes_ref[rows, :] = found
+        else:
+            for i in range(count // columns):
+                row = rows.start // columns + i
+                codes_out[row] = found[i * columns : (i + 1) * columns, :].T
         both = jnp.concatenate([found, found], axis=1)
         shifted = jnp.where(column == 0, 0.0, pltpu.roll(both, 1, 0))
         half = lax.broadcasted_iota(jnp.int32, (count, 128), 1) < 64
         wide[sweep, rows, :] = jnp.where(half, both, shifted).astype(BF16)
 
     def analyze(sweep):
+        if sweep == 0:
+            load_first.wait()
+            resid[first, :] = img[first, :] * weight[first, :]
         found = scores(first)
-        low_out[sweep] = found[:, 128:]
+        below_row = found[:, 128:192] + lift(found[:, 128:])[:, 64:]
+        half = columns // 2
+        low_out[sweep] = jnp.concatenate([below_row[:half], below_row[half:]], axis=1)
 
         @pl.when(me > 0)
         def _():
             low_copy(sweep).start()
 
         totals[first, :] = found[:, :128]
+        if sweep == 0:
+            load_rest.wait()
+            resid[columns:, :] = img[columns:, :] * weight[columns:, :]
         rest = scores(slice(columns, total_rows))
         totals[columns:, :] = rest[:, :128]
         upto = total_rows - columns
@@ -154,7 +183,9 @@
         def _():
             low_copy(sweep).wait_recv()
 
-        update(sweep, last, totals[last, :] + low_in[sweep])
+        came = low_in[sweep]
+        extra = jnp.concatenate([came[:, :64], came[:, 64:]], axis=0)
+        update(sweep, last, totals[last, :], extra)
 
         @pl.when(me < devices - 1)
         def _():
@@ -174,8 +205,8 @@
 
     analyze(0)
 
-    def rest_chunk(index, carry):
-        residual(0, slice(columns, total_rows), "rest", cut(index, width))
+    def rest_chunk(sweep, index, carry):
+        residual(sweep, slice(columns, total_rows), "rest", cut(index, width))
         return carry
 
     def first_chunk(index, carry):
@@ -187,16 +218,16 @@
         def _():
             wide_copy(sweep).wait_recv()
 
-    lax.fori_loop(0, features // width, rest_chunk, 0)
+    lax.fori_loop(0, features // width, functools.partial(rest_chunk, 0), 0)
     await_above(0)
     lax.fori_loop(0, features // width, first_chunk, 0)
     analyze(1)
+    lax.fori_loop(0, features // width, functools.partial(rest_chunk, 1), 0)
 
     chunk = features // quads if fused else features // 4
     own = chunk // QUAD
 
     def gradient(here):
-        residual(1, slice(columns, total_rows), "rest", here)
         residual(1, first, "first", here)
         codes = jnp.concatenate([fold(1, "first"), fold(1, "rest")], axis=0)
         found = lax.dot_general(
@@ -223,7 +254,7 @@
             )
 
         def far_copy(step):
-            owner = chunk_of(step, far, quads) * QUAD + 2 * side + core
+            owner = target_of(step, far, quads) * QUAD + 2 * side + core
             return pltpu.make_async_remote_copy(
                 far_out.at[step], far_in.at[step], far_send.at[step], far_recv.at[step], **to(owner)
             )
@@ -246,7 +277,11 @@
             return mine + side_in[step].astype(F32)
 
         def stage_far(step):
-            far_out[step] = summed(step).astype(BF16)
+            value = summed(step)
+            if quads == 4 and step == 1:
+                far_copy(0).wait_recv()
+                value = value + far_in[0].astype(F32)
+            far_out[step] = value.astype(BF16)
             far_copy(step).start()
 
         for step in range(quads):
@@ -259,7 +294,7 @@
         if quads >= 2:
             stage_far(quads - 2)
         result = summed(quads - 1)
-        for step in range(quads - 1):
+        for step in range(1 if quads == 4 else 0, quads - 1):
             far_copy(step).wait_recv()
             result = result + far_in[step].astype(F32)
         grad_ref[...] = result
@@ -279,6 +314,17 @@
             wide_copy(sweep).wait_send()
 
 
+def hand_on(codes_in, grad_in, codes_out, grad_out, sems):
+    moves = (
+        pltpu.make_async_copy(codes_in, codes_out, sems.at[0]),
+        pltpu.make_async_copy(grad_in, grad_out, sems.at[1]),
+    )
+    for move in moves:
+        move.start()
+    for move in moves:
+        move.wait()
+
+
 def local(devices, image, mask, dictionary, penalty):
     block_rows, columns, features = image.shape
     atoms = dictionary.shape[0]
@@ -287,26 +333,27 @@
     fused = devices % QUAD == 0 and features % (quads * 128) == 0 and features // devices % 16 == 0
     own = features // devices
     slots = (quads, own) if fused else (1, 16)
-    flat = jnp.transpose(dictionary, (1, 0, 2)).reshape(4 * atoms, features)
     dma, vmem = pltpu.SemaphoreType.DMA, pltpu.VMEM
     near, there = pl.BlockSpec(memory_space=pltpu.VMEM), pl.BlockSpec(memory_space=pl.ANY)
     codes, grad = pl.pallas_call(
         functools.partial(kernel, devices, block_rows, columns, fused),
         out_shape=(
-            jax.ShapeDtypeStruct((rows, atoms), F32),
+            jax.ShapeDtypeStruct((block_rows, atoms, columns), F32),
             jax.ShapeDtypeStruct((own if fused else features, 4 * atoms), F32),
         ),
         in_specs=[there, near, there, near],
         out_specs=(near, near),
         scratch_shapes=[
+            vmem((rows, atoms), F32),
+            vmem((atoms, 4, features), BF16),
             vmem((rows, features), BF16),
             vmem((4 * atoms, features), BF16),
             vmem((rows, features), BF16),
             vmem((rows, features), BF16),
             vmem((rows, 128), F32),
             vmem((rows, 128), F32),
-            vmem((2, columns, 128), F32),
-            vmem((2, columns, 128), F32),
+            vmem((2, columns // 2, 128), F32),
+            vmem((2, columns // 2, 128), F32),
             vmem((2, rows, 128), BF16),
             vmem((2, columns, 128), BF16),
             vmem((slots[0], QUAD * slots[1], 4 * atoms), F32),
@@ -316,7 +363,7 @@
             vmem((slots[0], slots[1], 4 * atoms), BF16),
             vmem((slots[0], slots[1], 4 * atoms), BF16),
             vmem((slots[0], slots[1], 4 * atoms), BF16),
-            dma, dma,
+            dma((2,)), dma,
             dma((2,)), dma((2,)), dma((2,)), dma((2,)),
             dma((slots[0],)), dma((slots[0],)), dma((slots[0],)),
             dma((slots[0],)), dma((slots[0],)), dma((slots[0],)),
@@ -324,10 +371,20 @@
         compiler_params=pltpu.CompilerParams(
             collective_id=0, has_side_effects=True, vmem_limit_bytes=56 * 1024 * 1024
         ),
-    )(image.reshape(rows, features), mask, flat, penalty.reshape(1, atoms))
+    )(image.reshape(rows, features), mask, dictionary, penalty.reshape(1, atoms))
     if not fused:
         grad = lax.psum_scatter(grad, "row", scatter_dimension=0, tiled=True)
-    return (codes.reshape(block_rows, columns, atoms), grad)
+    codes, grad = pl.pallas_call(
+        hand_on,
+        out_shape=(
+            jax.ShapeDtypeStruct(codes.shape, F32),
+            jax.ShapeDtypeStruct(grad.shape, F32),
+        ),
+        in_specs=[there, there],
+        out_specs=(there, there),
+        scratch_shapes=[dma((2,))],
+    )(codes, grad)
+    return (jnp.transpose(codes, (0, 2, 1)), grad)
 
 
 def solution(mesh):

time: 50.6 us -> 56.2 us (1.11)
  Pallas kernels: 43.3 us -> 55.4 us
  local copies, waits for them, and re-layouts: 6.43 us -> 0 us
    pallas_call x0 -> x1, Pallas kernels: none -> 12 us  [local(): pl.pallas_call(hand_on, out_shape=(jax.ShapeDtypeStruct(codes.shape, F32)...]
    unnamed x2 -> x0, local copies, waits for them, and re-layouts: 3.36 us -> none
    transpose x1 -> x0, local copies, waits for them, and re-layouts: 3.06 us -> none  [local(): flat = jnp.transpose(dictionary, (1, 0, 2)).reshape(4 * atoms, features)]
where the time goes in v2:
time: 56.2 us; the launch traced here: 56.1 us
  Pallas kernels  55.4 us (99%)
  between operations  0.64 us (1%)
    pallas_call x1, Pallas kernels, local(): pl.pallas_call(functools.partial(kernel, devices, block_rows, columns, fu...  43.4 us
    pallas_call x1, Pallas kernels, local(): pl.pallas_call(hand_on, out_shape=(jax.ShapeDtypeStruct(codes.shape, F32)...  12 us

profile of v2, /device:TPU:0, one launch (start us, length us, event | category | flops | bytes accessed | tf_op | source)
XLA Modules:
  0.0 56.1 jit_solution(14294831865300963347)
XLA Ops:
  0.6 43.4 %shard_map.59 = (f32[4,64,128]{2,1,0:T(8,128)}, f32[224,256]{1,0:T(8,128)}) custom-call(bf16[512,3584]{1,0:T(8,128)(2,1)} %bitcast.3, s32[4,2048]{1,0:T(4,128)} %mask_ref.1, bf16[64,4,3584]{2,1,0:T(4,128)(2,1)} %dict_hbm.1, f32[1,64]{1,0:T(1,128)} %bitcast.4), custom_call_target="tpu_custom_call" | custom-call | tf_op jit(solution)/shard_map/pallas_call | solution.py:338
  44.0 12.0 %shard_map.60 = (f32[4,64,128]{2,1,0:T(8,128)}, f32[224,256]{1,0:T(8,128)}) custom-call(f32[4,64,128]{2,1,0:T(8,128)} %get-tuple-element.6.codes_in, f32[224,256]{1,0:T(8,128)} %get-tuple-element.7.grad_in), custom_call_target="tpu_custom_call" | custom-call | tf_op jit(solution)/shard_map/pallas_call | solution.py:377

commit v3 on v2

--- a/solution.py
+++ b/solution.py
@@ -108,8 +108,7 @@
     lax.fori_loop(0, features // width, start_chunk, 0)
     load_dict.wait()
     atoms = raw.shape[0]
-    for quarter in range(4):
-        dic[quarter * atoms : (quarter + 1) * atoms, :] = raw[:, quarter, :]
+    dic[...] = jnp.swapaxes(raw[...], 0, 1).reshape(4 * atoms, features)
     above = (me + devices - 1) // devices
     below = (2 * devices - 2 - me) // devices
     pl.semaphore_wait(barrier, above + below + (peers if fused else 0))
@@ -314,15 +313,9 @@
             wide_copy(sweep).wait_send()
 
 
-def hand_on(codes_in, grad_in, codes_out, grad_out, sems):
-    moves = (
-        pltpu.make_async_copy(codes_in, codes_out, sems.at[0]),
-        pltpu.make_async_copy(grad_in, grad_out, sems.at[1]),
-    )
-    for move in moves:
-        move.start()
-    for move in moves:
-        move.wait()
+def hand_on(codes_in, grad_in, codes_out, grad_out):
+    codes_out[...] = codes_in[...]
+    grad_out[...] = grad_in[...]
 
 
 def local(devices, image, mask, dictionary, penalty):
@@ -380,9 +373,8 @@
             jax.ShapeDtypeStruct(codes.shape, F32),
             jax.ShapeDtypeStruct(grad.shape, F32),
         ),
-        in_specs=[there, there],
-        out_specs=(there, there),
-        scratch_shapes=[dma((2,))],
+        in_specs=[near, near],
+        out_specs=(near, near),
     )(codes, grad)
     return (jnp.transpose(codes, (0, 2, 1)), grad)
 

time: 56.2 us -> 43 us (0.77)
  Pallas kernels: 55.4 us -> 42.1 us
    pallas_call x1, Pallas kernels: 12 us -> 1.74 us  [local(): pl.pallas_call(hand_on, out_shape=(jax.ShapeDtypeStruct(codes.shape, F32)...]
    pallas_call x1, Pallas kernels: 43.4 us -> 40.4 us  [local(): pl.pallas_call(functools.partial(kernel, devices, block_rows, columns, fu...]
where the time goes in v3:
time: 43 us; the launch traced here: 42.8 us
  Pallas kernels  42.1 us (98%)
  between operations  0.64 us (1%)
    pallas_call x1, Pallas kernels, local(): pl.pallas_call(functools.partial(kernel, devices, block_rows, columns, fu...  40.4 us
    pallas_call x1, Pallas kernels, local(): pl.pallas_call(hand_on, out_shape=(jax.ShapeDtypeStruct(codes.shape, F32)...  1.74 us

profile of v3, /device:TPU:0, one launch (start us, length us, event | category | flops | bytes accessed | tf_op | source)
XLA Modules:
  0.0 42.8 jit_solution(18040875498073739089)
XLA Ops:
  0.6 40.4 %shard_map.59 = (f32[4,64,128]{2,1,0:T(8,128)}, f32[224,256]{1,0:T(8,128)}) custom-call(bf16[512,3584]{1,0:T(8,128)(2,1)} %bitcast.3, s32[4,2048]{1,0:T(4,128)} %mask_ref.1, bf16[64,4,3584]{2,1,0:T(4,128)(2,1)} %dict_hbm.1, f32[1,64]{1,0:T(1,128)} %bitcast.4), custom_call_target="tpu_custom_call" | custom-call | tf_op jit(solution)/shard_map/pallas_call | solution.py:331
  41.0 1.7 %shard_map.60 = (f32[4,64,128]{2,1,0:T(8,128)}, f32[224,256]{1,0:T(8,128)}) custom-call(f32[4,64,128]{2,1,0:T(8,128)} %get-tuple-element.6.codes_in, f32[224,256]{1,0:T(8,128)} %get-tuple-element.7.grad_in), custom_call_target="tpu_custom_call" | custom-call | tf_op jit(solution)/shard_map/pallas_call | solution.py:370

commit v4 on v3

--- a/solution.py
+++ b/solution.py
@@ -287,11 +287,9 @@
             stage_core(step)
             if step >= 1:
                 stage_side(step - 1)
-            if step >= 2:
-                stage_far(step - 2)
         stage_side(quads - 1)
-        if quads >= 2:
-            stage_far(quads - 2)
+        for step in range(quads - 1):
+            stage_far(step)
         result = summed(quads - 1)
         for step in range(1 if quads == 4 else 0, quads - 1):
             far_copy(step).wait_recv()

time: 43 us -> 42.1 us (0.979)
  Pallas kernels: 42.1 us -> 41 us
    pallas_call x1, Pallas kernels: 40.4 us -> 39.3 us  [local(): pl.pallas_call(functools.partial(kernel, devices, block_rows, columns, fu...]
where the time goes in v4:
time: 42.1 us; the launch traced here: 41.7 us
  Pallas kernels  41 us (97%)
  between operations  0.64 us (2%)
    pallas_call x1, Pallas kernels, local(): pl.pallas_call(functools.partial(kernel, devices, block_rows, columns, fu...  39.3 us
    pallas_call x1, Pallas kernels, local(): pl.pallas_call(hand_on, out_shape=(jax.ShapeDtypeStruct(codes.shape, F32)...  1.74 us

profile of v4, /device:TPU:0, one launch (start us, length us, event | category | flops | bytes accessed | tf_op | source)
XLA Modules:
  0.0 41.7 jit_solution(142185048184091044)
XLA Ops:
  0.6 39.3 %shard_map.59 = (f32[4,64,128]{2,1,0:T(8,128)}, f32[224,256]{1,0:T(8,128)}) custom-call(bf16[512,3584]{1,0:T(8,128)(2,1)} %bitcast.3, s32[4,2048]{1,0:T(4,128)} %mask_ref.1, bf16[64,4,3584]{2,1,0:T(4,128)(2,1)} %dict_hbm.1, f32[1,64]{1,0:T(1,128)} %bitcast.4), custom_call_target="tpu_custom_call" | custom-call | tf_op jit(solution)/shard_map/pallas_call | solution.py:329
  39.9 1.7 %shard_map.60 = (f32[4,64,128]{2,1,0:T(8,128)}, f32[224,256]{1,0:T(8,128)}) custom-call(f32[4,64,128]{2,1,0:T(8,128)} %get-tuple-element.6.codes_in, f32[224,256]{1,0:T(8,128)} %get-tuple-element.7.grad_in), custom_call_target="tpu_custom_call" | custom-call | tf_op jit(solution)/shard_map/pallas_call | solution.py:368
